TPU v7x, 512 devices: a whole 4x4x16 slice. The times are simulated.
512 devices in a mesh: dp: 4 (over y_hi, core), seq: 128 (over x, y_lo, z).
Axes of the slice: x: 4, y: 4 (y_hi: 2, y_lo: 2; y = y_hi * 2 + y_lo), z: 16, core: 2. Of those that a mesh axis runs over, the one named last changes fastest.
Arguments:
- clip_frames: bfloat16 [512, 16, 128, 128], P(('dp', 'seq')), parts along dimension 0, may hold values from -6 to 6
- cotangent: bfloat16 [512, 16, 128, 128], P(('dp', 'seq')), parts along dimension 0, may hold values from -6 to 6
- spatial_weight: bfloat16 [3, 3, 16, 16], replicated, may hold values from -0.5 to 0.5
- temporal_weight: bfloat16 [3, 3, 16, 16], replicated, may hold values from -0.4375 to 0.4375
Outputs:
- block_output: bfloat16 [512, 16, 128, 128], P(('dp', 'seq')), parts along dimension 0
- clip_grad: bfloat16 [512, 16, 128, 128], P(('dp', 'seq')), parts along dimension 0
- spatial_grad: float32 [12, 3, 16, 16], P('dp'), parts along dimension 0
- temporal_grad: float32 [12, 3, 16, 16], P('dp'), parts along dimension 0
There are 4 independent parts, one for each index of `dp`. A program takes and returns all parts, laid end to end along the dimension named above; an argument that names none is the same for every part. Nothing has to cross between parts.
All inputs are finite; a program needn't handle non-finite values.
Results may differ from a plain program's by a relative error of at most 0.0071.
Values may be sent and summed in bfloat16 or wider, within the bound.
A program may use at most 64 MiB of HBM per device.

v0:
```python
import math
import jax
import jax.numpy as jnp
from jax import lax
from jax.sharding import PartitionSpec as P


def shifted(values, row_step, col_step):
    row_count = values.shape[2]
    col_count = values.shape[3]
    padded = jnp.pad(values, ((0, 0), (0, 0), (1, 1), (1, 1)))
    return padded[
        :, :, 1 + row_step : 1 + row_step + row_count, 1 + col_step : 1 + col_step + col_count
    ]


def patches_of(values, orient):
    return jnp.concatenate(
        [shifted(values, orient * (a - 1), orient * (b - 1)) for a in range(3) for b in range(3)],
        axis=1,
    )


def time_shift(values, offset):
    length = values.shape[0]
    if offset > 0:
        return jnp.concatenate([values[offset:], jnp.zeros_like(values[:offset])], axis=0)
    if offset < 0:
        return jnp.concatenate([jnp.zeros_like(values[offset:]), values[:offset]], axis=0)
    return values


def silu_slope(preact):
    sigma = jax.nn.sigmoid(preact)
    return sigma * (1.0 + preact * (1.0 - sigma))


def temporal_forward(tiles, temporal_weight):
    states = [tiles]
    for layer in range(temporal_weight.shape[0]):
        dilation = 2**layer
        current = states[-1]
        branch = current.astype(jnp.float32)
        for tap in range(3):
            branch = branch + jnp.einsum(
                "tchw,cd->tdhw",
                time_shift(current, (tap - 1) * dilation),
                temporal_weight[layer, tap],
                preferred_element_type=jnp.float32,
            )
        states.append(branch.astype(jnp.bfloat16))
    return states


def body(clip_frames, cotangent, spatial_weight, temporal_weight):
    frames_dev, channels, row_count, col_count = clip_frames.shape
    layer_count = temporal_weight.shape[0]
    factor = 1.0 / math.sqrt(frames_dev * lax.axis_size("seq") * row_count * col_count)
    patches = patches_of(clip_frames, 1)
    flat_weight = spatial_weight.reshape(9 * channels, channels)
    preact = jnp.einsum("fkhw,kd->fdhw", patches, flat_weight, preferred_element_type=jnp.float32)
    activated = jax.nn.silu(preact).astype(jnp.bfloat16)
    tiles = lax.all_to_all(activated, "seq", split_axis=2, concat_axis=0, tiled=True)
    states = temporal_forward(tiles, temporal_weight)
    block_output = lax.all_to_all(states[-1], "seq", split_axis=0, concat_axis=2, tiled=True)
    grad_tiles = lax.all_to_all(cotangent, "seq", split_axis=2, concat_axis=0, tiled=True)
    gradient = grad_tiles
    layer_terms = [None] * layer_count
    for layer in reversed(range(layer_count)):
        dilation = 2**layer
        current = states[layer]
        local_term = jnp.stack(
            [
                jnp.einsum(
                    "tchw,tdhw->cd",
                    time_shift(current, (tap - 1) * dilation),
                    gradient,
                    preferred_element_type=jnp.float32,
                )
                for tap in range(3)
            ]
        )
        layer_terms[layer] = lax.psum(local_term, "seq")
        total = gradient.astype(jnp.float32)
        for tap in range(3):
            total = total + jnp.einsum(
                "tdhw,cd->tchw",
                time_shift(gradient, -(tap - 1) * dilation),
                temporal_weight[layer, tap],
                preferred_element_type=jnp.float32,
            )
        gradient = total.astype(jnp.bfloat16)
    grad_frames = lax.all_to_all(gradient, "seq", split_axis=0, concat_axis=2, tiled=True)
    slope = (grad_frames.astype(jnp.float32) * silu_slope(preact)).astype(jnp.bfloat16)
    spatial_term = jnp.einsum(
        "fkhw,fdhw->kd", patches, slope, preferred_element_type=jnp.float32
    ).reshape(3, 3, channels, channels)
    spatial_total = lax.psum(spatial_term, "seq")
    temporal_total = jnp.stack(layer_terms)
    mixing = spatial_weight.transpose(2, 0, 1, 3).reshape(channels, 9 * channels)
    clip_grad = jnp.einsum(
        "fkhw,ck->fchw", patches_of(slope, -1), mixing, preferred_element_type=jnp.float32
    ).astype(jnp.bfloat16)
    return (block_output, clip_grad, spatial_total * factor, temporal_total * factor)


def solution(mesh):
    placed = (P(("dp", "seq"), None, None, None), P(("dp", "seq"), None, None, None), P(), P())
    return jax.shard_map(
        body,
        mesh=mesh,
        in_specs=placed,
        out_specs=(
            P(("dp", "seq"), None, None, None),
            P(("dp", "seq"), None, None, None),
            P("dp", None, None, None),
            P("dp", None, None, None),
        ),
        check_vma=False,
    )
```

profile of v0, /device:TPU:16, one launch (start us, length us, event | category | flops | bytes accessed | tf_op | source)
XLA Modules:
  0.0 781.2 jit_solution(5370593056510770013)
XLA Ops:
  0.6 1.4 copy.73
  2.0 54.3 %all_to_all.57 = bf16[1,16,128,128]{3,1,0,2:T(8,128)(2,1)S(1)} all-to-all(bf16[1,16,128,128]{3,1,0,2:T(8,128)(2,1)S(1)} %copy.73), channel_id=1, replica_groups=mesh['dp'=4,'seq'=128] {'seq'}, dimensions={2} | all-to-all | bytes 1048576 | tf_op jit(solution)/shard_map/all_to_all | solution.py:66
  56.5 1.0 convolution_bitcast_fusion.6
  59.7 1.1 fusion.35
  60.8 6.2 all-to-all-start.3
  67.4 1.0 fusion.40
  69.4 1.0 fusion.42
  70.4 1.0 fusion.43
  71.4 1.2 constant_dynamic-update-slice_fusion
  72.6 1.0 fusion.44
  73.6 1.1 fusion.45
  75.6 1.0 fusion.47
  76.7 23.6 %all-to-all-done.3 = bf16[128,16,1,128]{3,1,2,0:T(8,128)(2,1)S(1)} async-done(((bf16[128,16,1,128]{3,1,2,0:T(8,128)(2,1)}), bf16[128,16,1,128]{3,1,2,0:T(8,128)(2,1)S(1)}, u32[]{:S(2)}, u32[]{:S(2)}) %all-to-all-start.3) | async-done | bytes 524320 | tf_op jit(solution)/shard_map/all_to_all | solution.py:93
  100.3 3.9 fusion.39
  104.3 6.7 all-to-all-start
  111.1 3.7 fusion.56
  118.4 25.7 %all-to-all-done = bf16[1,16,128,128]{3,1,0,2:T(8,128)(2,1)S(1)} async-done(((bf16[1,16,128,128]{3,1,0,2:T(8,128)(2,1)}), bf16[1,16,128,128]{3,1,0,2:T(8,128)(2,1)S(1)}, u32[]{:S(2)}, u32[]{:S(2)}) %all-to-all-start) | async-done | bytes 524320 | tf_op jit(solution)/shard_map/all_to_all | solution.py:63
  148.0 1.2 fusion.34
  149.2 7.3 all-to-all-start.1
  156.8 1.4 convolution_bitcast_fusion.26
  158.2 1.4 convolution_bitcast_fusion.21
  159.6 1.4 convolution_bitcast_fusion.23
  162.3 615.6 %all-reduce.14 = (f32[3,3,16,16]{3,2,0,1:T(8,128)S(1)}, f32[1,3,16,16]{3,2,0,1:T(8,128)S(1)}, f32[1,3,16,16]{3,2,0,1:T(8,128)S(1)}, f32[1,3,16,16]{3,2,0,1:T(8,128)S(1)}) all-reduce(f32[3,3,16,16]{3,2,0,1:T(8,128)S(1)} %bitcast.469, f32[1,3,16,16]{3,2,0,1:T(8,128)S(1)} %maximum_bitcast_fusion.2, ...), channel_id=1, replica_groups=mesh['dp'=4,'seq'=128] {'seq'}, use_global_device_ids=true, to_apply=%region_0.1 | all-reduce | flops 4608 | bytes 36864 | tf_op jit(solution)/shard_map/psum | solution.py:98
  779.2 2.0 copy.87
  (71 shorter events, 14.9 us)
Async XLA Ops:
  0.6 56.8 %copy-start.8 = (bf16[3,3,16,16]{3,2,1,0:T(8,128)(2,1)S(1)}, bf16[3,3,16,16]{3,2,1,0:T(8,128)(2,1)}, u32[]{:S(2)}) copy-start(bf16[3,3,16,16]{3,2,1,0:T(8,128)(2,1)} %param.7) | copy-start | bytes 13828
  59.0 8.0 %copy-start.7 = (bf16[1,16,128,128]{3,2,1,0:T(8,128)(2,1)S(1)}, bf16[1,16,128,128]{3,2,1,0:T(8,128)(2,1)}, u32[]{:S(2)}) copy-start(bf16[1,16,128,128]{3,2,1,0:T(8,128)(2,1)} %param.4) | copy-start | bytes 1572868
  60.8 39.5 %all-to-all-start.3 = ((bf16[128,16,1,128]{3,1,2,0:T(8,128)(2,1)}), bf16[128,16,1,128]{3,1,2,0:T(8,128)(2,1)S(1)}, u32[]{:S(2)}, u32[]{:S(2)}) async-start(bf16[128,16,1,128]{3,1,2,0:T(8,128)(2,1)} %fusion.35), calls=%async_computation.3 | async-start | bytes 1048576 | tf_op jit(solution)/shard_map/all_to_all | solution.py:93
  67.4 32.9 %copy-start.9 = (bf16[3,3,16,16]{3,2,1,0:T(8,128)(2,1)S(1)}, bf16[3,3,16,16]{3,2,1,0:T(8,128)(2,1)}, u32[]{:S(2)}) copy-start(bf16[3,3,16,16]{3,2,1,0:T(8,128)(2,1)} %param.6) | copy-start | bytes 13828
  104.3 39.8 %all-to-all-start = ((bf16[1,16,128,128]{3,1,0,2:T(8,128)(2,1)}), bf16[1,16,128,128]{3,1,0,2:T(8,128)(2,1)S(1)}, u32[]{:S(2)}, u32[]{:S(2)}) async-start(bf16[1,16,128,128]{3,1,0,2:T(8,128)(2,1)} %get-tuple-element.21), calls=%async_computation | async-start | bytes 1048576 | tf_op jit(solution)/shard_map/all_to_all | solution.py:63
  144.2 1.5 copy-start
  145.7 1.5 copy-start.1
  145.7 1.5 copy-start.2
  146.9 0.8 copy-start.5
  146.9 1.1 copy-start.3
  149.2 630.0 %all-to-all-start.1 = ((bf16[128,16,1,128]{3,1,2,0:T(8,128)(2,1)}), bf16[128,16,1,128]{3,1,2,0:T(8,128)(2,1)}, u32[]{:S(2)}, u32[]{:S(2)}) async-start(bf16[128,16,1,128]{3,1,2,0:T(8,128)(2,1)} %fusion.34), calls=%async_computation.1 | async-start | bytes 1048576 | tf_op jit(solution)/shard_map/all_to_all | solution.py:65
  156.5 4.8 copy-start.6
  156.5 5.1 copy-start.4
where the time goes:
time: 782 us; the launch traced here: 781 us
  blocking collectives  670 us (86%)
  waiting for transfers between devices  49.3 us (6%)
  matrix products  22.2 us (3%)
  starting transfers between devices  20.2 us (3%)
  local copies, waits for them, and re-layouts  18.5 us (2%)
    psum x1, blocking collectives, body(): spatial_total = lax.psum(spatial_term, 'seq')  616 us
    all_to_all x1, blocking collectives, body(): lax.all_to_all(cotangent, 'seq', split_axis=2, concat_axis=0, tiled=True)  54.3 us
    all_to_all x1, waiting for transfers between devices, body(): lax.all_to_all(activated, 'seq', split_axis=2, concat_axis=0, tiled=True)  25.7 us
    all_to_all x1, waiting for transfers between devices, body(): lax.all_to_all(gradient, 'seq', split_axis=0, concat_axis=2, tiled=True)  23.6 us
    unnamed x42, local copies, waits for them, and re-layouts  16.2 us
  transfers between devices with their start and end apart: 3, of which 2 were waited for; matrix products, arithmetic and copies ran while one was open for 3% of the time, Pallas kernels for 0%

commit v1 on v0

--- a/solution.py
+++ b/solution.py
@@ -95,7 +95,7 @@
     spatial_term = jnp.einsum(
         "fkhw,fdhw->kd", patches, slope, preferred_element_type=jnp.float32
     ).reshape(3, 3, channels, channels)
-    spatial_total = lax.psum(spatial_term, "seq")
+    spatial_total = jnp.sum(lax.all_gather(spatial_term, "seq"), axis=0)
     temporal_total = jnp.stack(layer_terms)
     mixing = spatial_weight.transpose(2, 0, 1, 3).reshape(channels, 9 * channels)
     clip_grad = jnp.einsum(

time: 782 us -> 804 us (1.028)
  between operations: 1.02 us -> 14.4 us
    unnamed x42 -> x38, local copies, waits for them, and re-layouts: 16.2 us -> 14.9 us
  transfers between devices with their start and end apart: 3 -> 4, of which waited for: 2 -> 2; matrix products, arithmetic and copies ran while one was open for 3% -> 4% of each run, Pallas kernels for 0% -> 0%
where the time goes in v1:
time: 804 us; the launch traced here: 803 us
  blocking collectives  673 us (84%)
  waiting for transfers between devices  48.8 us (6%)
  matrix products  23.2 us (3%)
  starting transfers between devices  20.2 us (3%)
  local copies, waits for them, and re-layouts  17.8 us (2%)
  between operations  14.4 us (2%)
    psum x1, blocking collectives, body(): layer_terms[layer] = lax.psum(local_term, 'seq')  619 us
    all_to_all x1, blocking collectives, body(): lax.all_to_all(cotangent, 'seq', split_axis=2, concat_axis=0, tiled=True)  54.3 us
    all_to_all x1, waiting for transfers between devices, body(): lax.all_to_all(activated, 'seq', split_axis=2, concat_axis=0, tiled=True)  25.1 us
    all_to_all x1, waiting for transfers between devices, body(): lax.all_to_all(gradient, 'seq', split_axis=0, concat_axis=2, tiled=True)  23.6 us
  transfers between devices with their start and end apart: 4, of which 2 were waited for; matrix products, arithmetic and copies ran while one was open for 4% of the time, Pallas kernels for 0%

profile of v1, /device:TPU:16, one launch (start us, length us, event | category | flops | bytes accessed | tf_op | source)
XLA Modules:
  0.0 803.3 jit_solution(6494352535721859480)
XLA Ops:
  7.2 1.4 copy.73
  8.6 54.3 %all_to_all.57 = bf16[1,16,128,128]{3,1,0,2:T(8,128)(2,1)S(1)} all-to-all(bf16[1,16,128,128]{3,1,0,2:T(8,128)(2,1)S(1)} %copy.73), channel_id=1, replica_groups=mesh['dp'=4,'seq'=128] {'seq'}, dimensions={2} | all-to-all | bytes 1048576 | tf_op jit(solution)/shard_map/all_to_all | solution.py:66
  66.2 1.1 fusion.37
  67.3 6.2 all-to-all-start.3
  73.9 1.0 fusion.45
  75.9 1.1 fusion.47
  77.0 1.0 fusion.48
  78.0 1.2 constant_dynamic-update-slice_fusion
  80.2 1.0 fusion.50
  82.2 1.0 fusion.52
  83.2 23.6 %all-to-all-done.3 = bf16[128,16,1,128]{3,1,2,0:T(8,128)(2,1)S(1)} async-done(((bf16[128,16,1,128]{3,1,2,0:T(8,128)(2,1)}), bf16[128,16,1,128]{3,1,2,0:T(8,128)(2,1)S(1)}, u32[]{:S(2)}, u32[]{:S(2)}) %all-to-all-start.3) | async-done | bytes 524320 | tf_op jit(solution)/shard_map/all_to_all | solution.py:93
  106.9 3.9 fusion.44
  110.8 6.5 all-to-all-start
  117.7 3.7 fusion.41
  125.6 25.1 %all-to-all-done = bf16[1,16,128,128]{3,1,0,2:T(8,128)(2,1)S(1)} async-done(((bf16[1,16,128,128]{3,1,0,2:T(8,128)(2,1)}), bf16[1,16,128,128]{3,1,0,2:T(8,128)(2,1)S(1)}, u32[]{:S(2)}, u32[]{:S(2)}) %all-to-all-start) | async-done | bytes 524320 | tf_op jit(solution)/shard_map/all_to_all | solution.py:63
  154.3 1.2 fusion.36
  155.8 7.3 all-to-all-start.1
  163.4 1.4 convolution_bitcast_fusion.24
  164.8 1.4 convolution_bitcast_fusion.23
  166.2 1.4 convolution_bitcast_fusion.21
  167.5 1.4 convolution_bitcast_fusion.20
  169.9 618.9 %all-reduce.14 = (f32[1,3,16,16]{3,2,1,0:T(8,128)S(1)}, f32[1,3,16,16]{3,2,1,0:T(8,128)S(1)}, f32[1,3,16,16]{3,2,1,0:T(8,128)S(1)}) all-reduce(f32[1,3,16,16]{3,2,1,0:T(8,128)S(1)} %get-tuple-element.34, f32[1,3,16,16]{3,2,1,0:T(8,128)S(1)} %get-tuple-element.33, ...), channel_id=1, replica_groups=mesh['dp'=4,'seq'=128] {'seq'}, use_global_device_ids=true, to_apply=%region_3.4 | all-reduce | flops 2304 | bytes 18432 | tf_op jit(solution)/shard_map/psum | solution.py:83
  789.5 4.4 reduce_sum.9
  794.5 2.0 copy.88
  (71 shorter events, 17.5 us)
Async XLA Ops:
  7.2 56.8 %copy-start.7 = (bf16[3,3,16,16]{3,2,1,0:T(8,128)(2,1)S(1)}, bf16[3,3,16,16]{3,2,1,0:T(8,128)(2,1)}, u32[]{:S(2)}) copy-start(bf16[3,3,16,16]{3,2,1,0:T(8,128)(2,1)} %param.7) | copy-start | bytes 13828
  65.6 8.0 copy-start.6
  67.3 39.5 %all-to-all-start.3 = ((bf16[128,16,1,128]{3,1,2,0:T(8,128)(2,1)}), bf16[128,16,1,128]{3,1,2,0:T(8,128)(2,1)S(1)}, u32[]{:S(2)}, u32[]{:S(2)}) async-start(bf16[128,16,1,128]{3,1,2,0:T(8,128)(2,1)} %fusion.37), calls=%async_computation.3 | async-start | bytes 1048576 | tf_op jit(solution)/shard_map/all_to_all | solution.py:93
  73.9 32.9 %copy-start.8 = (bf16[3,3,16,16]{3,2,1,0:T(8,128)(2,1)S(1)}, bf16[3,3,16,16]{3,2,1,0:T(8,128)(2,1)}, u32[]{:S(2)}) copy-start(bf16[3,3,16,16]{3,2,1,0:T(8,128)(2,1)} %param.6) | copy-start | bytes 13828
  110.8 39.9 %all-to-all-start = ((bf16[1,16,128,128]{3,1,0,2:T(8,128)(2,1)}), bf16[1,16,128,128]{3,1,0,2:T(8,128)(2,1)S(1)}, u32[]{:S(2)}, u32[]{:S(2)}) async-start(bf16[1,16,128,128]{3,1,0,2:T(8,128)(2,1)} %get-tuple-element.20), calls=%async_computation | async-start | bytes 1048576 | tf_op jit(solution)/shard_map/all_to_all | solution.py:63
  117.3 672.2 %all-gather.3.cloned.1.call-start = ((), (), s32[]{:S(2)}) async-start(), calls=%async_computation.4 | async-start | bytes 9510912 | tf_op jit(solution)/shard_map/all_gather | solution.py:98
  150.8 1.5 copy-start
  152.0 1.5 copy-start.1
  152.0 1.5 copy-start.2
  153.2 0.8 copy-start.3
  153.2 1.1 copy-start.5
  155.8 638.7 %all-to-all-start.1 = ((bf16[128,16,1,128]{3,1,2,0:T(8,128)(2,1)}), bf16[128,16,1,128]{3,1,2,0:T(8,128)(2,1)}, u32[]{:S(2)}, u32[]{:S(2)}) async-start(bf16[128,16,1,128]{3,1,2,0:T(8,128)(2,1)} %fusion.36), calls=%async_computation.1 | async-start | bytes 1048576 | tf_op jit(solution)/shard_map/all_to_all | solution.py:65
  163.1 5.8 copy-start.4
Sparse Core Ops, SparseCore 0:
  122.1 611.9 all-gather.2
